TPU v7x, 32 devices: a whole 2x2x4 slice. The times are simulated.
32 devices in a mesh: ctx: 8 (over z, y), head: 4 (over x, core).
Axes of the slice: x: 2, y: 2, z: 4, core: 2. Of those that a mesh axis runs over, the one named last changes fastest.
Arguments:
- queries: bfloat16 [8, 512, 3072], P('ctx', None, 'head'), may hold values from -5 to 5
- key_rows: bfloat16 [8, 512, 3072], P('ctx', None, 'head'), may hold values from -5 to 5
- value_rows: bfloat16 [8, 512, 3072], P('ctx', None, 'head'), may hold values from -6 to 6
- out_grad: bfloat16 [8, 512, 3072], P('ctx', None, 'head'), may hold values from -6 to 6
- head_kind: int32 [24], replicated, may hold values from 0 to 1, as said below
- frame_band: int32 [24], replicated, may hold values from 1 to 7, as said below
Outputs:
- attended: bfloat16 [8, 512, 3072], P('ctx', None, 'head')
- query_grad: bfloat16 [8, 512, 3072], P('ctx', None, 'head')
- key_grad: bfloat16 [8, 512, 3072], P('ctx', None, 'head')
- value_grad: bfloat16 [8, 512, 3072], P('ctx', None, 'head')
Inputs may be any that keep to these rules, and one draw needn't show every extreme that they name: `head_kind`: exactly 8 entries are 1. `frame_band`: entries of spatial heads are not used; some temporal head has the value 8 - 1.
All inputs are finite; a program needn't handle non-finite values.
Results may differ from a plain program's by a relative error of at most 0.024.
Values may be sent and summed in bfloat16 or wider, within the bound.
No kernel may reach another device: no remote copies, remote signals or barrier semaphores. Data moves between devices by JAX's collectives and lax.ppermute only.
A program may use at most 64 MiB of HBM per device.

v0:
```python
import functools
import math

import jax
import jax.numpy as jnp
from jax import lax
from jax.experimental import pallas as pl
from jax.experimental.pallas import tpu as pltpu
from jax.sharding import PartitionSpec as P

DH = 128
SCALE = DH ** (-0.5)
SPATIAL, TEMPORAL = 1, 0
MASKED = -1e30
SCALE_LOG2 = SCALE * math.log2(math.e)
F32 = jnp.float32
BF16 = jnp.bfloat16
MIB = 1024 * 1024


def head_at(kind_ref, first_ref, heads, kind, slot):
    found, seen = jnp.int32(0), jnp.int32(0)
    for head in range(heads):
        hit = kind_ref[first_ref[0] + head] == kind
        found = jnp.where(jnp.logical_and(hit, seen == slot), jnp.int32(head), found)
        seen = seen + hit.astype(jnp.int32)
    return found


def dot_nt(a, b):
    return lax.dot_general(a, b, (((1,), (1,)), ((), ())), preferred_element_type=F32)


def dot_nn(a, b):
    return lax.dot_general(a, b, (((1,), (0,)), ((), ())), preferred_element_type=F32)


def dot_tn(a, b):
    return lax.dot_general(a, b, (((0,), (0,)), ((), ())), preferred_element_type=F32)


def params(mib=32):
    return pltpu.CompilerParams(
        dimension_semantics=("arbitrary",), vmem_limit_bytes=mib * MIB
    )


def cost(flops, moved):
    return pl.CostEstimate(flops=int(flops), bytes_accessed=int(moved), transcendentals=0)


def column_spec(count, heads, kind):
    return pl.BlockSpec((count, DH), lambda i, *refs: (0, head_at(*refs[:2], heads, kind, i)))


def head_columns(kind_ref, first_ref, heads, kind, slot):
    return pl.ds(pl.multiple_of(head_at(kind_ref, first_ref, heads, kind, slot) * DH, DH), DH)


def staged_copies(triples, in_sems, out_sems):
    loads = [pltpu.make_async_copy(x, y, in_sems.at[i]) for i, (x, y, _) in enumerate(triples)]
    stores = [pltpu.make_async_copy(y, z, out_sems.at[i]) for i, (_, y, z) in enumerate(triples)]
    for load in loads:
        load.start()
    for load, store in zip(loads, stores):
        load.wait()
        store.start()
    for store in stores:
        store.wait()


def whole_params():
    return pltpu.CompilerParams(vmem_limit_bytes=62 * MIB)


def pack_spatial(kinds, first, arrays, slots, heads, after):
    frames, rows, _ = arrays[0].shape
    count = len(arrays)
    total = slots * count

    def kernel(kind_ref, first_ref, *refs):
        ins, outs = refs[:count], refs[-3 - count // 2 : -3]
        stage, in_sems, out_sems = refs[-3:]
        triples = []
        for slot in range(slots):
            cols = head_columns(kind_ref, first_ref, heads, SPATIAL, slot)
            for place, ref in enumerate(ins):
                target = outs[place // 2].at[slot, place % 2]
                triples.append((ref.at[:, :, cols], stage.at[slot, place], target))
        staged_copies(triples, in_sems, out_sems)

    return pl.pallas_call(
        kernel,
        out_shape=[jax.ShapeDtypeStruct((slots, 2, frames, rows, DH), BF16)] * (count // 2),
        in_specs=[pl.BlockSpec(memory_space=pltpu.SMEM)] * 2
        + [pl.BlockSpec(memory_space=pl.ANY)] * (count + len(after)),
        out_specs=[pl.BlockSpec(memory_space=pl.ANY)] * (count // 2),
        scratch_shapes=[
            pltpu.VMEM((slots, count, frames, rows, DH), BF16),
            pltpu.SemaphoreType.DMA((total,)),
            pltpu.SemaphoreType.DMA((total,)),
        ],
        compiler_params=whole_params(),
        cost_estimate=cost(0, 4 * total * frames * rows * DH),
        name="pack_spatial",
    )(kinds, first, *arrays, *after)


def pack_temporal(kinds, first, arrays, slots, heads):
    frames, rows, _ = arrays[0].shape
    total = 4 * slots

    def kernel(kind_ref, first_ref, *refs):
        ins, (out, stage, in_sems, out_sems) = refs[:4], refs[4:]
        triples = []
        for slot in range(slots):
            cols = head_columns(kind_ref, first_ref, heads, TEMPORAL, slot)
            for place, ref in enumerate(ins):
                triples.append(
                    (ref.at[:, :, cols], stage.at[slot, place], out.at[:, place, slot])
                )
        staged_copies(triples, in_sems, out_sems)

    return pl.pallas_call(
        kernel,
        out_shape=jax.ShapeDtypeStruct((frames, 4, slots, rows, DH), BF16),
        in_specs=[pl.BlockSpec(memory_space=pltpu.SMEM)] * 2
        + [pl.BlockSpec(memory_space=pl.ANY)] * 4,
        out_specs=pl.BlockSpec(memory_space=pl.ANY),
        scratch_shapes=[
            pltpu.VMEM((slots, 4, frames, rows, DH), BF16),
            pltpu.SemaphoreType.DMA((total,)),
            pltpu.SemaphoreType.DMA((total,)),
        ],
        compiler_params=whole_params(),
        cost_estimate=cost(0, 4 * total * frames * rows * DH),
        name="pack_temporal",
    )(kinds, first, *arrays)


def temporal(kinds, first, bands, rows_in, heads):
    frames, _, slots, rows, _ = rows_in.shape
    group = 16
    size = frames * group

    def frame_at(place):
        half = frames // 2
        return place + (place == half - 1).astype(jnp.int32) - (place == half).astype(jnp.int32)

    def kernel(kind_ref, first_ref, band_ref, rows_ref, result_ref, held, made, in_sems, out_sems):
        def load(slot):
            return pltpu.make_async_copy(rows_ref.at[:, :, slot], held.at[slot], in_sems.at[slot])

        def store(slot):
            return pltpu.make_async_copy(
                made.at[slot], result_ref.at[:, :, slot], out_sems.at[slot]
            )

        for slot in range(slots):
            load(slot).start()

        def work(members):
            for slot in members:
                load(slot).wait()
            some_heads(
                kind_ref, first_ref, band_ref,
                [(slot, held.at[slot], made.at[slot]) for slot in members],
            )
            for slot in members:
                store(slot).start()

        if slots > 1:

            @pl.loop(0, slots // 2)
            def _(pair):
                work([2 * pair, 2 * pair + 1])

        if slots % 2:
            work([slots - 1])
        for slot in range(slots):
            store(slot).wait()

    def some_heads(kind_ref, first_ref, band_ref, members):
        row = lax.broadcasted_iota(jnp.int32, (size, size), 0)
        col = lax.broadcasted_iota(jnp.int32, (size, size), 1)
        same = lax.rem(row, group) == lax.rem(col, group)
        apart = jnp.abs(frame_at(lax.div(row, group)) - frame_at(lax.div(col, group)))
        distance = jnp.where(same, apart, frames)
        parts = [slice(start, start + group) for start in range(0, rows, group)]
        allowed, qs, ks, vs, gs = [], [], [], [], []
        for slot, in_ref, _ in members:
            head = head_at(kind_ref, first_ref, heads, TEMPORAL, slot)
            band = jnp.minimum(band_ref[first_ref[0] + head], frames - 1)
            allowed += [distance <= band] * len(parts)
            for place, rows_of in enumerate((qs, ks, vs, gs)):
                rows_of += [in_ref[:, place, part].reshape(size, DH) for part in parts]
        scores = [
            jnp.where(ok, dot_nt(k, q), MASKED) for ok, q, k in zip(allowed, qs, ks)
        ]
        dprobs = [dot_nt(v, g) for g, v in zip(gs, vs)]
        raised = [
            jnp.exp2((x - jnp.max(x, axis=0, keepdims=True)) * SCALE_LOG2) for x in scores
        ]
        weights = [x * (1.0 / jnp.sum(x, axis=0, keepdims=True)) for x in raised]
        probs = [x.astype(BF16) for x in weights]
        deltas = [jnp.sum(w * dp, axis=0, keepdims=True) for w, dp in zip(weights, dprobs)]
        dscores = [
            (w * (dp - delta) * SCALE).astype(BF16)
            for w, dp, delta in zip(weights, dprobs, deltas)
        ]
        results = (
            [dot_tn(x, v).astype(BF16) for x, v in zip(probs, vs)],
            [dot_tn(x, k).astype(BF16) for x, k in zip(dscores, ks)],
            [dot_nn(x, q).astype(BF16) for x, q in zip(dscores, qs)],
            [dot_nn(x, g).astype(BF16) for x, g in zip(probs, gs)],
        )
        for place, result in enumerate(results):
            targets = [(out_ref, part) for _, _, out_ref in members for part in parts]
            for (out_ref, part), value in zip(targets, result):
                out_ref[:, place, part] = value.reshape(frames, group, DH)

    block = (slots, frames, 4, rows, DH)
    return pl.pallas_call(
        kernel,
        out_shape=jax.ShapeDtypeStruct(rows_in.shape, BF16),
        in_specs=[pl.BlockSpec(memory_space=pltpu.SMEM)] * 3
        + [pl.BlockSpec(memory_space=pl.ANY)],
        out_specs=pl.BlockSpec(memory_space=pl.ANY),
        scratch_shapes=[
            pltpu.VMEM(block, BF16),
            pltpu.VMEM(block, BF16),
            pltpu.SemaphoreType.DMA((slots,)),
            pltpu.SemaphoreType.DMA((slots,)),
        ],
        compiler_params=whole_params(),
        cost_estimate=cost(1e10, 4 * rows_in.size),
        name="temporal",
    )(kinds, first, bands, rows_in)


def spatial(kinds, first, frame, arrays, prior, heads):
    count = arrays[0].shape[0]
    slots = prior.shape[0]
    chunk = min(count, 128)

    def kernel(
        kind_ref, first_ref, frame_ref, q_ref, k_ref, v_ref, g_ref, prior_ref,
        out_ref, qgrad_ref, own_ref, stats_ref,
    ):
        has_prior = frame_ref[0] > 0
        k, v = k_ref[...], v_ref[...]
        k_prior, v_prior = prior_ref[0, 0], prior_ref[0, 1]
        own_ref[...] = jnp.zeros_like(own_ref)

        @pl.loop(0, count // chunk)
        def _(step):
            part = pl.ds(pl.multiple_of(step * chunk, chunk), chunk)
            q, g = q_ref[part], g_ref[part]
            own = dot_nt(k, q)
            before = jnp.where(has_prior, dot_nt(k_prior, q), MASKED)
            top = jnp.maximum(
                jnp.max(own, axis=0, keepdims=True), jnp.max(before, axis=0, keepdims=True)
            )
            own, before = (jnp.exp2((x - top) * SCALE_LOG2) for x in (own, before))
            total = jnp.sum(own, axis=0, keepdims=True) + jnp.sum(before, axis=0, keepdims=True)
            inverse = 1.0 / total
            own, before = own * inverse, before * inverse
            own_dp, before_dp = dot_nt(v, g), dot_nt(v_prior, g)
            delta = jnp.sum(own * own_dp, axis=0, keepdims=True) + jnp.sum(
                before * before_dp, axis=0, keepdims=True
            )
            own_prob, before_prob = own.astype(BF16), before.astype(BF16)
            own_ds = (own * (own_dp - delta) * SCALE).astype(BF16)
            before_ds = (before * (before_dp - delta) * SCALE).astype(BF16)
            out_ref[part] = (dot_tn(own_prob, v) + dot_tn(before_prob, v_prior)).astype(BF16)
            qgrad_ref[part] = (dot_tn(own_ds, k) + dot_tn(before_ds, k_prior)).astype(BF16)
            own_ref[0, 0] += dot_nn(own_ds, q)
            own_ref[0, 1] += dot_nn(own_prob, g)
            stats_ref[0, 0:1, part] = top * SCALE + jnp.log(total)
            stats_ref[0, 1:2, part] = delta

    columns = column_spec(count, heads, SPATIAL)
    pair = pl.BlockSpec((1, 2, count, DH), lambda i, *refs: (i, 0, 0, 0))
    whole = jax.ShapeDtypeStruct((count, heads * DH), BF16)
    return pl.pallas_call(
        kernel,
        out_shape=[
            whole,
            whole,
            jax.ShapeDtypeStruct(prior.shape, F32),
            jax.ShapeDtypeStruct((slots, 2, count), F32),
        ],
        grid_spec=pltpu.PrefetchScalarGridSpec(
            num_scalar_prefetch=3,
            grid=(slots,),
            in_specs=[columns] * 4 + [pair],
            out_specs=[
                columns, columns, pair, pl.BlockSpec((1, 2, count), lambda i, *refs: (i, 0, 0))
            ],
        ),
        compiler_params=params(24),
        cost_estimate=cost(2e11, 16 * slots * count * DH),
        name="spatial",
    )(kinds, first, frame, *arrays, prior)


def spatial_next(kinds, first, k, v, following, stats, own, heads):
    slots, _, count, _ = own.shape
    chunk = min(count, 256)

    def kernel(
        kind_ref, first_ref, k_in, v_in, next_in, stats_in, own_in, k_out, v_out,
        kv_ref, next_ref, stats_ref, own_ref, made_ref, in_sems, out_sems,
    ):
        def loads(slot):
            cols = head_columns(kind_ref, first_ref, heads, SPATIAL, slot)
            pairs = [
                (k_in.at[:, cols], kv_ref.at[slot, 0]),
                (v_in.at[:, cols], kv_ref.at[slot, 1]),
                (next_in.at[slot], next_ref.at[slot]),
                (stats_in.at[slot], stats_ref.at[slot]),
                (own_in.at[slot], own_ref.at[slot]),
            ]
            return [
                pltpu.make_async_copy(*pair, in_sems.at[slot, i]) for i, pair in enumerate(pairs)
            ]

        def stores(slot):
            cols = head_columns(kind_ref, first_ref, heads, SPATIAL, slot)
            return [
                pltpu.make_async_copy(made_ref.at[slot, i], out.at[:, cols], out_sems.at[slot, i])
                for i, out in enumerate((k_out, v_out))
            ]

        for slot in range(slots):
            for copy in loads(slot):
                copy.start()

        @pl.loop(0, slots)
        def _(slot):
            for copy in loads(slot):
                copy.wait()
            q, g = next_ref[slot, 0], next_ref[slot, 1]
            lse, delta = stats_ref[slot, 0:1] * math.log2(math.e), stats_ref[slot, 1:2]
            parts = [slice(start, start + chunk) for start in range(0, count, chunk)]
            scores = [dot_nt(kv_ref[slot, 0, part], q) for part in parts]
            dprobs = [dot_nt(kv_ref[slot, 1, part], g) for part in parts]
            weights = [jnp.exp2(x * SCALE_LOG2 - lse) for x in scores]
            slopes = [(w * (x - delta)).astype(BF16) for w, x in zip(weights, dprobs)]
            for part, weight, slope in zip(parts, weights, slopes):
                terms = dot_nn(slope, q) * SCALE, dot_nn(weight.astype(BF16), g)
                for i, term in enumerate(terms):
                    made_ref[slot, i, part] = (own_ref[slot, i, part] + term).astype(BF16)
            for copy in stores(slot):
                copy.start()

        for slot in range(slots):
            for copy in stores(slot):
                copy.wait()

    return pl.pallas_call(
        kernel,
        out_shape=[jax.ShapeDtypeStruct(k.shape, BF16)] * 2,
        in_specs=[pl.BlockSpec(memory_space=pltpu.SMEM)] * 2
        + [pl.BlockSpec(memory_space=pl.ANY)] * 5,
        out_specs=[pl.BlockSpec(memory_space=pl.ANY)] * 2,
        scratch_shapes=[
            pltpu.VMEM((slots, 2, count, DH), BF16),
            pltpu.VMEM((slots, 2, count, DH), BF16),
            pltpu.VMEM((slots, 2, count), F32),
            pltpu.VMEM((slots, 2, count, DH), F32),
            pltpu.VMEM((slots, 2, count, DH), BF16),
            pltpu.SemaphoreType.DMA((slots, 5)),
            pltpu.SemaphoreType.DMA((slots, 2)),
        ],
        compiler_params=pltpu.CompilerParams(vmem_limit_bytes=24 * MIB),
        cost_estimate=cost(8 * slots * count * count * DH, 20 * slots * count * DH),
        name="spatial_next",
    )(kinds, first, k, v, following, stats, own)


def unpack(kinds, first, rows_in, filled, heads):
    frames, _, slots, rows, _ = rows_in.shape
    count = frames * rows
    total = 4 * slots

    def kernel(kind_ref, first_ref, in_ref, *refs):
        outs, (stage, in_sems, out_sems) = refs[-7:-3], refs[-3:]
        triples = []
        for slot in range(slots):
            cols = head_columns(kind_ref, first_ref, heads, TEMPORAL, slot)
            for place, out in enumerate(outs):
                held = stage.at[slot, place]
                triples.append((in_ref.at[:, place, slot], held, out.at[:, :, cols]))
        staged_copies(triples, in_sems, out_sems)

    shape = (frames, rows, heads * DH)
    filled = [x.reshape(shape) for x in filled]
    outs = pl.pallas_call(
        kernel,
        out_shape=[jax.ShapeDtypeStruct(shape, BF16)] * 4,
        in_specs=[pl.BlockSpec(memory_space=pltpu.SMEM)] * 2
        + [pl.BlockSpec(memory_space=pl.ANY)] * (1 + len(filled)),
        out_specs=[pl.BlockSpec(memory_space=pl.ANY)] * 4,
        scratch_shapes=[
            pltpu.VMEM((slots, 4, frames, rows, DH), BF16),
            pltpu.SemaphoreType.DMA((total,)),
            pltpu.SemaphoreType.DMA((total,)),
        ],
        input_output_aliases={3 + place: place for place in range(len(filled))},
        compiler_params=pltpu.CompilerParams(vmem_limit_bytes=24 * MIB),
        cost_estimate=cost(0, 4 * rows_in.size),
        name="unpack",
    )(kinds, first, rows_in, *filled)
    return [x.reshape(count, heads * DH) for x in outs]


def passed_along(array, axis, by):
    length = lax.axis_size(axis)
    pairs = [(i, i + by) for i in range(length) if 0 <= i + by < length]
    return lax.ppermute(array, axis, pairs)


def behind(arrays, *others):
    return lax.optimization_barrier((tuple(arrays), others))[0]


def neighbour_rows(ahead, back, frame, results):
    length = lax.axis_size("ctx")
    even = lax.rem(frame[0], 2) == 0
    far = [(i, i - 1 if i % 2 == 0 else i + 1) for i in range(length)]
    far = [pair for pair in far if 0 <= pair[1] < length]
    near = [(i, i + 1 if i % 2 == 0 else i - 1) for i in range(length)]
    near = lax.ppermute(jnp.where(even, ahead, back), "ctx", near)
    far = lax.ppermute(jnp.where(even, back, ahead), "ctx", far)
    if results is not None:
        near, far = behind((near, far), results)
    return jnp.where(even, far, near), jnp.where(even, near, far)


def exchange_order(frames):
    half = frames // 2
    return [*range(half - 1), half, half - 1, *range(half + 1, frames)]


def branch(slots, heads, kinds, bands, first, frame, q, k, v, g):
    frames, rows, width = q.shape
    count = frames * rows
    others = heads - slots
    exchange = functools.partial(
        lax.all_to_all, axis_name="ctx", split_axis=0, concat_axis=0, tiled=True,
        axis_index_groups=[exchange_order(frames)],
    )
    flat = [x.reshape(count, width) for x in (q, k, v, g)]
    packed = []
    filled, results = (), None
    if slots > 0:
        packed = [pack_temporal(kinds, first, (q, k, v, g), slots, heads)]
        framed = exchange(*packed)
        results = temporal(kinds, first, bands, framed, heads)
        returned = exchange(results)
    if others > 0:
        ahead, back = pack_spatial(kinds, first, (k, v, q, g), others, heads, packed)
        arrived = neighbour_rows(ahead, back, frame, results)
        prior, following = (x.reshape(others, 2, count, DH) for x in arrived)
        attended, qgrad, own, stats = spatial(kinds, first, frame, flat, prior, heads)
        stats = passed_along(stats, "ctx", -1)
        grads = spatial_next(kinds, first, *flat[1:3], following, stats, own, heads)
        filled = (attended, qgrad, *grads)
    if slots > 0:
        filled = unpack(kinds, first, returned, filled, heads)
    return tuple(filled)


def body(queries, key_rows, value_rows, out_grad, head_kind, frame_band):
    frames = lax.axis_size("ctx")
    count = queries.shape[1]
    heads = queries.shape[2] // DH
    first = lax.axis_index("head").astype(jnp.int32) * heads
    frame = lax.axis_index("ctx").astype(jnp.int32)
    offset = jnp.arange(head_kind.shape[0], dtype=jnp.int32) - first
    here = jnp.logical_and(offset >= 0, offset < heads)
    slots = jnp.sum(jnp.logical_and(here, head_kind == TEMPORAL).astype(jnp.int32))
    arrays = [
        x.reshape(frames, count // frames, heads * DH)
        for x in (queries, key_rows, value_rows, out_grad)
    ]
    outs = lax.switch(
        slots,
        [functools.partial(branch, n, heads) for n in range(heads + 1)],
        head_kind, frame_band, first.reshape(1), frame.reshape(1), *arrays,
    )
    return tuple(out.reshape(queries.shape) for out in outs)


def solution(mesh):
    rows = P("ctx", None, "head")
    return jax.shard_map(
        body,
        mesh=mesh,
        in_specs=(rows, rows, rows, rows, P(), P()),
        out_specs=(rows, rows, rows, rows),
        check_vma=False,
    )
```

profile of v0, /device:TPU:14, one launch (start us, length us, event | category | flops | bytes accessed | tf_op | source)
XLA Modules:
  0.0 123.5 jit_solution(1251810760189913122)
XLA Ops:
  0.6 1.3 %fusion = s32[]{:T(128)} fusion(s32[24]{0:T(128)} %param.17, s32[]{:T(128)} %mul.3), kind=kLoop, calls=%fused_computation.25 | loop fusion | flops 191 | bytes 104 | tf_op jit(solution)/shard_map/reduce_sum | solution.py:483
  2.6 120.7 %conditional.1 = (bf16[512,768]{1,0:T(8,128)(2,1)}, bf16[512,768]{1,0:T(8,128)(2,1)}, bf16[512,768]{1,0:T(8,128)(2,1)}, bf16[512,768]{1,0:T(8,128)(2,1)}) conditional(s32[]{:T(128)} %clamp.3, (bf16[1,512,768]{2,1,0:T(8,128)(2,1)}, bf16[1,512,768]{2,1,0:T(8,128)(2,1)}, bf16[1,512,768]{2,1,0:T(8,128)(2,1)}, ...), branch_computations={%region_1.2_spmd, %region_2.3_spmd, %region_3.4_spmd, %region_4.5_... | conditional | flops 211344801792 | bytes 58295016 | solution.py:488
  2.8 3.4 %pack_temporal.9.refs_4_ = bf16[8,4,4,64,128]{4,3,2,1,0:T(8,128)(2,1)} custom-call(s32[24]{0:T(128)} %get-tuple-element.269.kind_ref, s32[1]{0:T(128)} %get-tuple-element.270.first_ref, bf16[8,64,768]{2,1,0:T(8,128)(2,1)} %bitcast.177, bf16[8,64,768]{2,1,0:T(8,128)(2,1)} %bitcast.123, bf16[8,64,768]{2,1,0:T(8,128)(2,1)} %bitcast.152, ...), custom_call_target="tpu_custom_call" | custom-call | bytes 4194304 | tf_op jit(solution)/shard_map/cond/branch_4_fun/pack_temporal/pallas_call | solution.py:124
  6.2 0.0 copy-start.4
  6.2 0.0 copy-start.10
  6.2 0.0 copy-start.27
  6.3 6.4 %all-to-all-start.8 = ((bf16[8,4,4,64,128]{4,3,2,1,0:T(8,128)(2,1)}), bf16[8,4,4,64,128]{4,3,2,1,0:T(8,128)(2,1)}, u32[]{:S(2)}, u32[]{:S(2)}) async-start(bf16[8,4,4,64,128]{4,3,2,1,0:T(8,128)(2,1)} %pack_temporal.9.refs_4_), calls=%async_computation.8 | async-start | bytes 4194304 | tf_op jit(solution)/shard_map/cond/branch_4_fun/all_to_all | solution.py:459
  12.6 0.0 copy-done.4
  12.6 0.0 copy-done.10
  12.6 0.0 copy-done.27
  12.6 2.6 %pack_spatial.10 = (bf16[2,2,8,64,128]{4,3,2,1,0:T(8,128)(2,1)}, bf16[2,2,8,64,128]{4,3,2,1,0:T(8,128)(2,1)}) custom-call(s32[24]{0:T(128)S(1)} %copy-done.27, s32[1]{0:T(128)} %get-tuple-element.270.first_ref, bf16[8,64,768]{2,1,0:T(8,128)(2,1)S(1)} %bitcast.124, bf16[8,64,768]{2,1,0:T(8,128)(2,1)S(1)} %bitcast.153, bf16[8,64,768]{2,1,0:T(8,128)(2,1)} %bitcast.178, ...), custom_call_target="tpu_custom_call" | custom-call | bytes 2097152 | tf_op jit(solution)/shard_map/cond/branch_4_fun/pack_spatial/pallas_call | solution.py:92
  15.3 0.0 copy-start.33
  15.3 2.2 %broadcast_select_fusion.18 = (bf16[2,2,8,64,128]{4,3,2,1,0:T(8,128)(2,1)}, bf16[2,2,8,64,128]{4,3,2,1,0:T(8,128)(2,1)}) fusion(bf16[2,2,8,64,128]{4,3,2,1,0:T(8,128)(2,1)} %get-tuple-element.283, bf16[2,2,8,64,128]{4,3,2,1,0:T(8,128)(2,1)} %get-tuple-element.282, pred[]{:T(512)S(6)} %eq.18), kind=kLoop, calls=%fused_computation.18 | loop fusion | flops 524288 | bytes 2097153 | tf_op jit(solution)/shard_map/cond/branch_4_fun/jit(_where)/select_n | solution.py:435
  17.5 3.4 %collective-permute-start.13 = (bf16[2,2,8,64,128]{4,3,2,1,0:T(8,128)(2,1)}, bf16[2,2,8,64,128]{4,3,2,1,0:T(8,128)(2,1)}, u32[]{:S(2)}, u32[]{:S(2)}) collective-permute-start(bf16[2,2,8,64,128]{4,3,2,1,0:T(8,128)(2,1)} %get-tuple-element.364), channel_id=1, source_target_pairs={{4,8},{8,4},{12,16},{16,12},{20,24},{24,20},{5,9},{9,5},{13,17},{1... | collective-permute-start | bytes 1572872 | tf_op jit(solution)/shard_map/cond/branch_4_fun/ppermute | solution.py:435
  20.9 0.6 collective-permute-start.12
  21.5 39.5 %all-to-all-done.8.rows_ref = bf16[8,4,4,64,128]{4,3,2,1,0:T(8,128)(2,1)} async-done(((bf16[8,4,4,64,128]{4,3,2,1,0:T(8,128)(2,1)}), bf16[8,4,4,64,128]{4,3,2,1,0:T(8,128)(2,1)}, u32[]{:S(2)}, u32[]{:S(2)}) %all-to-all-start.8) | async-done | bytes 2097184 | tf_op jit(solution)/shard_map/cond/branch_4_fun/all_to_all | solution.py:459
  61.0 0.0 copy-done.33
  61.0 4.6 %temporal.9 = bf16[8,4,4,64,128]{4,3,2,1,0:T(8,128)(2,1)} custom-call(s32[24]{0:T(128)S(1)} %copy-done.27, s32[1]{0:T(128)} %get-tuple-element.270.first_ref, s32[24]{0:T(128)S(1)} %copy-done.33, bf16[8,4,4,64,128]{4,3,2,1,0:T(8,128)(2,1)} %all-to-all-done.8.rows_ref), custom_call_target="tpu_custom_call" | custom-call | flops 10000000000 | bytes 4194304 | tf_op jit(solution)/shard_map/cond/branch_4_fun/temporal/pallas_call | solution.py:223
  65.6 5.3 %all-to-all-start.9 = ((bf16[8,4,4,64,128]{4,3,2,1,0:T(8,128)(2,1)}), bf16[8,4,4,64,128]{4,3,2,1,0:T(8,128)(2,1)}, u32[]{:S(2)}, u32[]{:S(2)}) async-start(bf16[8,4,4,64,128]{4,3,2,1,0:T(8,128)(2,1)} %temporal.9), calls=%async_computation.9 | async-start | bytes 4194304 | tf_op jit(solution)/shard_map/cond/branch_4_fun/all_to_all | solution.py:461
  70.9 0.0 copy-start.16
  70.9 0.0 copy-start.22
  70.9 0.0 collective-permute-done.13
  70.9 0.0 collective-permute-done.12
  70.9 1.4 %broadcast_select_fusion.16 = (bf16[2,2,8,64,128]{4,3,2,1,0:T(8,128)(2,1)S(1)}, bf16[2,2,8,64,128]{4,3,2,1,0:T(8,128)(2,1)S(1)}) fusion(bf16[2,2,8,64,128]{4,3,2,1,0:T(8,128)(2,1)} %collective-permute-done.12, bf16[2,2,8,64,128]{4,3,2,1,0:T(8,128)(2,1)} %collective-permute-done.13, pred[]{:T(512)S(6)} %eq.18), kind=kLoop, calls=%fused_computation.16 | loop fusion | flops 524288 | bytes 2097153 | tf_op jit(solution)/shard_map/cond/branch_4_fun/jit(_where)/select_n | solution.py:438
  72.3 0.0 copy-done.16
  72.4 0.2 copy-done.22
  72.6 9.6 %spatial.10 = (bf16[512,768]{1,0:T(8,128)(2,1)}, bf16[512,768]{1,0:T(8,128)(2,1)}, f32[2,2,512,128]{3,2,1,0:T(8,128)S(1)}, f32[2,2,512]{2,1,0:T(2,128)S(1)}) custom-call(s32[24]{0:T(128)S(1)} %copy-done.27, s32[1]{0:T(128)} %get-tuple-element.270.first_ref, s32[1]{0:T(128)} %get-tuple-element.276.frame_ref, bf16[512,768]{1,0:T(8,128)(2,1)S(1)} %bitcast.179, ...), custom_call_target="tpu_custom_call" | custom-call | flops 199999995904 | bytes 2097152 | tf_op jit(solution)/shard_map/cond/branch_4_fun/spatial/pallas_call | solution.py:285
  82.2 2.5 %collective-permute-start.14 = (f32[2,2,512]{2,1,0:T(2,128)S(1)}, f32[2,2,512]{2,1,0:T(2,128)S(1)}, u32[]{:S(2)}, u32[]{:S(2)}) collective-permute-start(f32[2,2,512]{2,1,0:T(2,128)S(1)} %get-tuple-element.288), channel_id=1, source_target_pairs={{4,0},{8,4},{12,8},{16,12},{20,16},{24,20},{28,24},{5,1},{9,5},{13... | collective-permute-start | bytes 24584 | tf_op jit(solution)/shard_map/cond/branch_4_fun/ppermute | solution.py:421
  84.7 32.3 %collective-permute-done.14.stats_in = f32[2,2,512]{2,1,0:T(2,128)S(1)} collective-permute-done((f32[2,2,512]{2,1,0:T(2,128)S(1)}, f32[2,2,512]{2,1,0:T(2,128)S(1)}, u32[]{:S(2)}, u32[]{:S(2)}) %collective-permute-start.14) | collective-permute-done | bytes 8224 | tf_op jit(solution)/shard_map/cond/branch_4_fun/ppermute | solution.py:421
  117.1 3.1 %spatial_next.10 = (bf16[512,768]{1,0:T(8,128)(2,1)}, bf16[512,768]{1,0:T(8,128)(2,1)}) custom-call(s32[24]{0:T(128)S(1)} %copy-done.27, s32[1]{0:T(128)} %get-tuple-element.270.first_ref, bf16[512,768]{1,0:T(8,128)(2,1)S(1)} %bitcast.126, bf16[512,768]{1,0:T(8,128)(2,1)S(1)} %bitcast.155, bf16[2,2,512,128]{3,2,1,0:T(8,128)(2,1)S(1)} %bitcast.94, ...), custom_call_target="tpu_custom_call" | custom-call | flops 536870912 | bytes 2621440 | tf_op jit(solution)/shard_map/cond/branch_4_fun/spatial_next/pallas_call | solution.py:361
  120.2 0.0 all-to-all-done.9.in_ref
  120.2 3.1 %unpack.9 = (bf16[8,64,768]{2,1,0:T(8,128)(2,1)}, bf16[8,64,768]{2,1,0:T(8,128)(2,1)}, bf16[8,64,768]{2,1,0:T(8,128)(2,1)}, bf16[8,64,768]{2,1,0:T(8,128)(2,1)}) custom-call(s32[24]{0:T(128)S(1)} %copy-done.27, s32[1]{0:T(128)} %get-tuple-element.270.first_ref, ...), custom_call_target="tpu_custom_call", output_to_operand_aliasing={{0}: (3, {}), {1}: (4, {}), {2}: (5, {}), {3}: (6, {})} | custom-call | bytes 4194304 | tf_op jit(solution)/shard_map/cond/branch_4_fun/unpack/pallas_call | solution.py:399
Async XLA Ops:
  6.2 6.4 %copy-start.4 = (bf16[1,512,768]{2,1,0:T(8,128)(2,1)S(1)}, bf16[1,512,768]{2,1,0:T(8,128)(2,1)}, u32[]{:S(2)}) copy-start(bf16[1,512,768]{2,1,0:T(8,128)(2,1)} %get-tuple-element.278) | copy-start | bytes 2359300 | tf_op jit(solution)/shard_map/cond
  6.2 6.4 %copy-start.10 = (bf16[1,512,768]{2,1,0:T(8,128)(2,1)S(1)}, bf16[1,512,768]{2,1,0:T(8,128)(2,1)}, u32[]{:S(2)}) copy-start(bf16[1,512,768]{2,1,0:T(8,128)(2,1)} %get-tuple-element.279) | copy-start | bytes 2359300 | tf_op jit(solution)/shard_map/cond
  6.2 6.4 %copy-start.27 = (s32[24]{0:T(128)S(1)}, s32[24]{0:T(128)}, u32[]{:S(2)}) copy-start(s32[24]{0:T(128)} %get-tuple-element.269.kind_ref) | copy-start | bytes 292 | tf_op jit(solution)/shard_map/cond
  6.3 54.8 %all-to-all-start.8 = ((bf16[8,4,4,64,128]{4,3,2,1,0:T(8,128)(2,1)}), bf16[8,4,4,64,128]{4,3,2,1,0:T(8,128)(2,1)}, u32[]{:S(2)}, u32[]{:S(2)}) async-start(bf16[8,4,4,64,128]{4,3,2,1,0:T(8,128)(2,1)} %pack_temporal.9.refs_4_), calls=%async_computation.8 | async-start | bytes 4194304 | tf_op jit(solution)/shard_map/cond/branch_4_fun/all_to_all | solution.py:459
  15.3 45.7 %copy-start.33 = (s32[24]{0:T(128)S(1)}, s32[24]{0:T(128)}, u32[]{:S(2)}) copy-start(s32[24]{0:T(128)} %get-tuple-element.271.band_ref) | copy-start | bytes 292 | tf_op jit(solution)/shard_map/cond
  17.5 53.4 %collective-permute-start.13 = (bf16[2,2,8,64,128]{4,3,2,1,0:T(8,128)(2,1)}, bf16[2,2,8,64,128]{4,3,2,1,0:T(8,128)(2,1)}, u32[]{:S(2)}, u32[]{:S(2)}) collective-permute-start(bf16[2,2,8,64,128]{4,3,2,1,0:T(8,128)(2,1)} %get-tuple-element.364), channel_id=1, source_target_pairs={{4,8},{8,4},{12,16},{16,12},{20,24},{24,20},{5,9},{9,5},{13,17},{1... | collective-permute-start | bytes 1572872 | tf_op jit(solution)/shard_map/cond/branch_4_fun/ppermute | solution.py:435
  20.9 50.0 %collective-permute-start.12 = (bf16[2,2,8,64,128]{4,3,2,1,0:T(8,128)(2,1)}, bf16[2,2,8,64,128]{4,3,2,1,0:T(8,128)(2,1)}, u32[]{:S(2)}, u32[]{:S(2)}) collective-permute-start(bf16[2,2,8,64,128]{4,3,2,1,0:T(8,128)(2,1)} %get-tuple-element.365), channel_id=1, source_target_pairs={{0,4},{4,0},{8,12},{12,8},{16,20},{20,16},{24,28},{28,24},{1,5},{5... | collective-permute-start | bytes 1572872 | tf_op jit(solution)/shard_map/cond/branch_4_fun/ppermute | solution.py:434
  65.6 54.5 %all-to-all-start.9 = ((bf16[8,4,4,64,128]{4,3,2,1,0:T(8,128)(2,1)}), bf16[8,4,4,64,128]{4,3,2,1,0:T(8,128)(2,1)}, u32[]{:S(2)}, u32[]{:S(2)}) async-start(bf16[8,4,4,64,128]{4,3,2,1,0:T(8,128)(2,1)} %temporal.9), calls=%async_computation.9 | async-start | bytes 4194304 | tf_op jit(solution)/shard_map/cond/branch_4_fun/all_to_all | solution.py:461
  70.9 1.4 %copy-start.16 = (bf16[1,512,768]{2,1,0:T(8,128)(2,1)S(1)}, bf16[1,512,768]{2,1,0:T(8,128)(2,1)}, u32[]{:S(2)}) copy-start(bf16[1,512,768]{2,1,0:T(8,128)(2,1)} %get-tuple-element.277) | copy-start | bytes 2359300 | tf_op jit(solution)/shard_map/cond
  70.9 1.7 %copy-start.22 = (bf16[1,512,768]{2,1,0:T(8,128)(2,1)S(1)}, bf16[1,512,768]{2,1,0:T(8,128)(2,1)}, u32[]{:S(2)}) copy-start(bf16[1,512,768]{2,1,0:T(8,128)(2,1)} %get-tuple-element.280) | copy-start | bytes 2359300 | tf_op jit(solution)/shard_map/cond
  82.2 34.8 %collective-permute-start.14 = (f32[2,2,512]{2,1,0:T(2,128)S(1)}, f32[2,2,512]{2,1,0:T(2,128)S(1)}, u32[]{:S(2)}, u32[]{:S(2)}) collective-permute-start(f32[2,2,512]{2,1,0:T(2,128)S(1)} %get-tuple-element.288), channel_id=1, source_target_pairs={{4,0},{8,4},{12,8},{16,12},{20,16},{24,20},{28,24},{5,1},{9,5},{13... | collective-permute-start | bytes 24584 | tf_op jit(solution)/shard_map/cond/branch_4_fun/ppermute | solution.py:421
where the time goes:
time: 124 us; the launch traced here: 123 us
  waiting for transfers between devices  71.8 us (58%)
  Pallas kernels  26.5 us (21%)
  starting transfers between devices  18.1 us (15%)
  other arithmetic  4.93 us (4%)
  between operations  1.47 us (1%)
    all_to_all x1, waiting for transfers between devices, branch(): framed = exchange(*packed)  39.5 us
    ppermute x1, waiting for transfers between devices, passed_along(): return lax.ppermute(array, axis, pairs)  32.3 us
    pallas_call x1, Pallas kernels, spatial(): pl.pallas_call(kernel, out_shape=[whole, whole, jax.ShapeDtypeStruct(prio...  9.64 us
    all_to_all x1, starting transfers between devices, branch(): framed = exchange(*packed)  6.37 us
    all_to_all x1, starting transfers between devices, branch(): returned = exchange(results)  5.3 us
    pallas_call x1, Pallas kernels, temporal(): pl.pallas_call(kernel, out_shape=jax.ShapeDtypeStruct(rows_in.shape, BF16...  4.6 us
    pallas_call x1, Pallas kernels, pack_temporal(): pl.pallas_call(kernel, out_shape=jax.ShapeDtypeStruct((frames, 4, slots,...  3.36 us
    ppermute x1, starting transfers between devices, neighbour_rows(): far = lax.ppermute(jnp.where(even, back, ahead), 'ctx', far)  3.36 us
  transfers between devices with their start and end apart: 5, of which 2 were waited for; matrix products, arithmetic and copies ran while one was open for 3% of the time, Pallas kernels for 16%

commit v1 on v0

--- a/solution.py
+++ b/solution.py
@@ -148,23 +148,20 @@
         return place + (place == half - 1).astype(jnp.int32) - (place == half).astype(jnp.int32)
 
     def kernel(kind_ref, first_ref, band_ref, rows_ref, result_ref, held, made, in_sems, out_sems):
-        def load(slot):
-            return pltpu.make_async_copy(rows_ref.at[:, :, slot], held.at[slot], in_sems.at[slot])
+        load = pltpu.make_async_copy(rows_ref, held, in_sems.at[0])
 
         def store(slot):
             return pltpu.make_async_copy(
                 made.at[slot], result_ref.at[:, :, slot], out_sems.at[slot]
             )
 
-        for slot in range(slots):
-            load(slot).start()
+        load.start()
+        load.wait()
 
         def work(members):
-            for slot in members:
-                load(slot).wait()
             some_heads(
                 kind_ref, first_ref, band_ref,
-                [(slot, held.at[slot], made.at[slot]) for slot in members],
+                [(slot, held.at[:, :, slot], made.at[slot]) for slot in members],
             )
             for slot in members:
                 store(slot).start()
@@ -227,9 +224,9 @@
         + [pl.BlockSpec(memory_space=pl.ANY)],
         out_specs=pl.BlockSpec(memory_space=pl.ANY),
         scratch_shapes=[
+            pltpu.VMEM(rows_in.shape, BF16),
             pltpu.VMEM(block, BF16),
-            pltpu.VMEM(block, BF16),
-            pltpu.SemaphoreType.DMA((slots,)),
+            pltpu.SemaphoreType.DMA((1,)),
             pltpu.SemaphoreType.DMA((slots,)),
         ],
         compiler_params=whole_params(),

time: 124 us -> 136 us (1.097)
  the two profiles are of different devices: /device:TPU:14 before, /device:TPU:13 now
where the time goes in v1:
time: 136 us
  waiting for transfers between devices  90.2 us (66%)
  Pallas kernels  23.1 us (17%)
  starting transfers between devices  16.4 us (12%)
  other arithmetic  4.18 us (3%)
  between operations  1.47 us (1%)
    all_to_all x1, waiting for transfers between devices, branch(): framed = exchange(*packed)  47.4 us
    ppermute x1, waiting for transfers between devices, passed_along(): return lax.ppermute(array, axis, pairs)  42.8 us
    pallas_call x1, Pallas kernels, spatial(): pl.pallas_call(kernel, out_shape=[whole, whole, jax.ShapeDtypeStruct(prio...  5.97 us
    all_to_all x1, starting transfers between devices, branch(): framed = exchange(*packed)  5.81 us
    pallas_call x1, Pallas kernels, temporal(): pl.pallas_call(kernel, out_shape=jax.ShapeDtypeStruct(rows_in.shape, BF16...  5.54 us
    all_to_all x1, starting transfers between devices, branch(): returned = exchange(results)  4.98 us
    pallas_call x1, Pallas kernels, pack_temporal(): pl.pallas_call(kernel, out_shape=jax.ShapeDtypeStruct((frames, 4, slots,...  3.65 us
    pallas_call x1, Pallas kernels, unpack(): pl.pallas_call(kernel, out_shape=[jax.ShapeDtypeStruct(shape, BF16)] * 4,...  3.39 us
  transfers between devices with their start and end apart: 5, of which 2 were waited for; matrix products, arithmetic and copies ran while one was open for 2% of the time, Pallas kernels for 12%

profile of v1, /device:TPU:13, one launch (start us, length us, event | category | flops | bytes accessed | tf_op | source)
XLA Modules:
  0.0 135.8 jit_solution(8092804897901573283)
XLA Ops:
  0.6 1.3 fusion
  2.6 133.0 %conditional.1 = (bf16[512,768]{1,0:T(8,128)(2,1)}, bf16[512,768]{1,0:T(8,128)(2,1)}, bf16[512,768]{1,0:T(8,128)(2,1)}, bf16[512,768]{1,0:T(8,128)(2,1)}) conditional(s32[]{:T(128)} %clamp.3, (bf16[1,512,768]{2,1,0:T(8,128)(2,1)}, bf16[1,512,768]{2,1,0:T(8,128)(2,1)}, bf16[1,512,768]{2,1,0:T(8,128)(2,1)}, ...), branch_computations={%region_1.2_spmd, %region_2.3_spmd, %region_3.4_spmd, %region_4.5_... | conditional | flops 211344801792 | bytes 58295016 | solution.py:485
  2.8 3.6 %pack_temporal.10.refs_4_ = bf16[8,4,5,64,128]{4,3,2,1,0:T(8,128)(2,1)} custom-call(s32[24]{0:T(128)} %get-tuple-element.296.kind_ref, s32[1]{0:T(128)} %get-tuple-element.297.first_ref, bf16[8,64,768]{2,1,0:T(8,128)(2,1)} %bitcast.180, bf16[8,64,768]{2,1,0:T(8,128)(2,1)} %bitcast.127, bf16[8,64,768]{2,1,0:T(8,128)(2,1)} %bitcast.156, ...), custom_call_target="tpu_custom_call" | custom-call | bytes 5242880 | tf_op jit(solution)/shard_map/cond/branch_5_fun/pack_temporal/pallas_call | solution.py:124
  6.5 0.0 copy-start.5
  6.5 0.0 copy-start.11
  6.5 0.0 copy-start.28
  6.5 5.8 %all-to-all-start.10 = ((bf16[8,4,5,64,128]{4,3,2,1,0:T(8,128)(2,1)}), bf16[8,4,5,64,128]{4,3,2,1,0:T(8,128)(2,1)}, u32[]{:S(2)}, u32[]{:S(2)}) async-start(bf16[8,4,5,64,128]{4,3,2,1,0:T(8,128)(2,1)} %pack_temporal.10.refs_4_), calls=%async_computation.10 | async-start | bytes 5242880 | tf_op jit(solution)/shard_map/cond/branch_5_fun/all_to_all | solution.py:456
  12.3 0.0 copy-done.5
  12.3 0.0 copy-done.11
  12.3 0.0 copy-done.28
  12.4 0.0 copy-start.34
  12.4 2.4 %pack_spatial.11 = (bf16[1,2,8,64,128]{4,3,2,1,0:T(8,128)(2,1)}, bf16[1,2,8,64,128]{4,3,2,1,0:T(8,128)(2,1)}) custom-call(s32[24]{0:T(128)S(1)} %copy-done.28, s32[1]{0:T(128)} %get-tuple-element.297.first_ref, bf16[8,64,768]{2,1,0:T(8,128)(2,1)S(1)} %bitcast.128, bf16[8,64,768]{2,1,0:T(8,128)(2,1)S(1)} %bitcast.157, bf16[8,64,768]{2,1,0:T(8,128)(2,1)} %bitcast.181, ...), custom_call_target="tpu_custom_call" | custom-call | bytes 1048576 | tf_op jit(solution)/shard_map/cond/branch_5_fun/pack_spatial/pallas_call | solution.py:92
  14.8 1.9 %broadcast_select_fusion.22 = (bf16[1,2,8,64,128]{4,3,2,1,0:T(8,128)(2,1)}, bf16[1,2,8,64,128]{4,3,2,1,0:T(8,128)(2,1)}) fusion(bf16[1,2,8,64,128]{4,3,2,1,0:T(8,128)(2,1)} %get-tuple-element.310, bf16[1,2,8,64,128]{4,3,2,1,0:T(8,128)(2,1)} %get-tuple-element.309, pred[]{:T(512)S(6)} %eq.19), kind=kLoop, calls=%fused_computation.22 | loop fusion | flops 262144 | bytes 1048577 | tf_op jit(solution)/shard_map/cond/branch_5_fun/jit(_where)/select_n | solution.py:432
  16.6 3.1 %collective-permute-start.16 = (bf16[1,2,8,64,128]{4,3,2,1,0:T(8,128)(2,1)}, bf16[1,2,8,64,128]{4,3,2,1,0:T(8,128)(2,1)S(1)}, u32[]{:S(2)}, u32[]{:S(2)}) collective-permute-start(bf16[1,2,8,64,128]{4,3,2,1,0:T(8,128)(2,1)} %get-tuple-element.368), channel_id=1, source_target_pairs={{4,8},{8,4},{12,16},{16,12},{20,24},{24,20},{5,9},{9,5},{13,17},{1... | collective-permute-start | bytes 786440 | tf_op jit(solution)/shard_map/cond/branch_5_fun/ppermute | solution.py:432
  19.7 0.3 collective-permute-start.15
  20.1 47.4 %all-to-all-done.10.rows_ref = bf16[8,4,5,64,128]{4,3,2,1,0:T(8,128)(2,1)} async-done(((bf16[8,4,5,64,128]{4,3,2,1,0:T(8,128)(2,1)}), bf16[8,4,5,64,128]{4,3,2,1,0:T(8,128)(2,1)}, u32[]{:S(2)}, u32[]{:S(2)}) %all-to-all-start.10) | async-done | bytes 2621472 | tf_op jit(solution)/shard_map/cond/branch_5_fun/all_to_all | solution.py:456
  67.5 0.0 copy-done.34
  67.5 5.5 %temporal.10 = bf16[8,4,5,64,128]{4,3,2,1,0:T(8,128)(2,1)} custom-call(s32[24]{0:T(128)S(1)} %copy-done.28, s32[1]{0:T(128)} %get-tuple-element.297.first_ref, s32[24]{0:T(128)S(1)} %copy-done.34, bf16[8,4,5,64,128]{4,3,2,1,0:T(8,128)(2,1)} %all-to-all-done.10.rows_ref), custom_call_target="tpu_custom_call" | custom-call | flops 10000000000 | bytes 5242880 | tf_op jit(solution)/shard_map/cond/branch_5_fun/temporal/pallas_call | solution.py:220
  73.0 0.0 copy-start.17
  73.0 5.0 %all-to-all-start.11 = ((bf16[8,4,5,64,128]{4,3,2,1,0:T(8,128)(2,1)}), bf16[8,4,5,64,128]{4,3,2,1,0:T(8,128)(2,1)}, u32[]{:S(2)}, u32[]{:S(2)}) async-start(bf16[8,4,5,64,128]{4,3,2,1,0:T(8,128)(2,1)} %temporal.10), calls=%async_computation.11 | async-start | bytes 5242880 | tf_op jit(solution)/shard_map/cond/branch_5_fun/all_to_all | solution.py:458
  78.0 0.0 collective-permute-done.16
  78.0 0.0 collective-permute-done.15
  78.0 1.0 broadcast_select_fusion.20
  79.0 0.0 copy-done.17
  79.1 6.0 %spatial.11 = (bf16[512,768]{1,0:T(8,128)(2,1)}, bf16[512,768]{1,0:T(8,128)(2,1)}, f32[1,2,512,128]{3,2,1,0:T(8,128)S(1)}, f32[1,2,512]{2,1,0:T(2,128)S(1)}) custom-call(s32[24]{0:T(128)S(1)} %copy-done.28, s32[1]{0:T(128)} %get-tuple-element.297.first_ref, s32[1]{0:T(128)} %get-tuple-element.303.frame_ref, bf16[512,768]{1,0:T(8,128)(2,1)S(1)} %bitcast.182, ...), custom_call_target="tpu_custom_call" | custom-call | flops 199999995904 | bytes 1048576 | tf_op jit(solution)/shard_map/cond/branch_5_fun/spatial/pallas_call | solution.py:282
  85.0 2.2 %collective-permute-start.17 = (f32[1,2,512]{2,1,0:T(2,128)S(1)}, f32[1,2,512]{2,1,0:T(2,128)S(1)}, u32[]{:S(2)}, u32[]{:S(2)}) collective-permute-start(f32[1,2,512]{2,1,0:T(2,128)S(1)} %get-tuple-element.315), channel_id=1, source_target_pairs={{4,0},{8,4},{12,8},{16,12},{20,16},{24,20},{28,24},{5,1},{9,5},{13... | collective-permute-start | bytes 12296 | tf_op jit(solution)/shard_map/cond/branch_5_fun/ppermute | solution.py:418
  87.2 42.8 %collective-permute-done.17.stats_in = f32[1,2,512]{2,1,0:T(2,128)S(1)} collective-permute-done((f32[1,2,512]{2,1,0:T(2,128)S(1)}, f32[1,2,512]{2,1,0:T(2,128)S(1)}, u32[]{:S(2)}, u32[]{:S(2)}) %collective-permute-start.17) | collective-permute-done | bytes 4128 | tf_op jit(solution)/shard_map/cond/branch_5_fun/ppermute | solution.py:418
  130.0 2.2 %spatial_next.11 = (bf16[512,768]{1,0:T(8,128)(2,1)}, bf16[512,768]{1,0:T(8,128)(2,1)}) custom-call(s32[24]{0:T(128)S(1)} %copy-done.28, s32[1]{0:T(128)} %get-tuple-element.297.first_ref, bf16[512,768]{1,0:T(8,128)(2,1)S(1)} %bitcast.130, bf16[512,768]{1,0:T(8,128)(2,1)S(1)} %bitcast.159, bf16[1,2,512,128]{3,2,1,0:T(8,128)(2,1)S(1)} %bitcast.98, ...), custom_call_target="tpu_custom_call" | custom-call | flops 268435456 | bytes 1310720 | tf_op jit(solution)/shard_map/cond/branch_5_fun/spatial_next/pallas_call | solution.py:358
  132.2 0.0 all-to-all-done.11.in_ref
  132.2 3.4 %unpack.10 = (bf16[8,64,768]{2,1,0:T(8,128)(2,1)}, bf16[8,64,768]{2,1,0:T(8,128)(2,1)}, bf16[8,64,768]{2,1,0:T(8,128)(2,1)}, bf16[8,64,768]{2,1,0:T(8,128)(2,1)}) custom-call(s32[24]{0:T(128)S(1)} %copy-done.28, s32[1]{0:T(128)} %get-tuple-element.297.first_ref, ...), custom_call_target="tpu_custom_call", output_to_operand_aliasing={{0}: (3, {}), {1}: (4, {}), {2}: (5, {}), {3}: (6, {})} | custom-call | bytes 5242880 | tf_op jit(solution)/shard_map/cond/branch_5_fun/unpack/pallas_call | solution.py:396
Async XLA Ops:
  6.5 5.8 %copy-start.5 = (bf16[1,512,768]{2,1,0:T(8,128)(2,1)S(1)}, bf16[1,512,768]{2,1,0:T(8,128)(2,1)}, u32[]{:S(2)}) copy-start(bf16[1,512,768]{2,1,0:T(8,128)(2,1)} %get-tuple-element.305) | copy-start | bytes 2359300 | tf_op jit(solution)/shard_map/cond
  6.5 5.8 %copy-start.11 = (bf16[1,512,768]{2,1,0:T(8,128)(2,1)S(1)}, bf16[1,512,768]{2,1,0:T(8,128)(2,1)}, u32[]{:S(2)}) copy-start(bf16[1,512,768]{2,1,0:T(8,128)(2,1)} %get-tuple-element.306) | copy-start | bytes 2359300 | tf_op jit(solution)/shard_map/cond
  6.5 5.8 %copy-start.28 = (s32[24]{0:T(128)S(1)}, s32[24]{0:T(128)}, u32[]{:S(2)}) copy-start(s32[24]{0:T(128)} %get-tuple-element.296.kind_ref) | copy-start | bytes 292 | tf_op jit(solution)/shard_map/cond
  6.5 60.9 %all-to-all-start.10 = ((bf16[8,4,5,64,128]{4,3,2,1,0:T(8,128)(2,1)}), bf16[8,4,5,64,128]{4,3,2,1,0:T(8,128)(2,1)}, u32[]{:S(2)}, u32[]{:S(2)}) async-start(bf16[8,4,5,64,128]{4,3,2,1,0:T(8,128)(2,1)} %pack_temporal.10.refs_4_), calls=%async_computation.10 | async-start | bytes 5242880 | tf_op jit(solution)/shard_map/cond/branch_5_fun/all_to_all | solution.py:456
  12.4 55.1 %copy-start.34 = (s32[24]{0:T(128)S(1)}, s32[24]{0:T(128)}, u32[]{:S(2)}) copy-start(s32[24]{0:T(128)} %get-tuple-element.298.band_ref) | copy-start | bytes 292 | tf_op jit(solution)/shard_map/cond
  16.6 61.4 %collective-permute-start.16 = (bf16[1,2,8,64,128]{4,3,2,1,0:T(8,128)(2,1)}, bf16[1,2,8,64,128]{4,3,2,1,0:T(8,128)(2,1)S(1)}, u32[]{:S(2)}, u32[]{:S(2)}) collective-permute-start(bf16[1,2,8,64,128]{4,3,2,1,0:T(8,128)(2,1)} %get-tuple-element.368), channel_id=1, source_target_pairs={{4,8},{8,4},{12,16},{16,12},{20,24},{24,20},{5,9},{9,5},{13,17},{1... | collective-permute-start | bytes 786440 | tf_op jit(solution)/shard_map/cond/branch_5_fun/ppermute | solution.py:432
  19.7 58.3 %collective-permute-start.15 = (bf16[1,2,8,64,128]{4,3,2,1,0:T(8,128)(2,1)}, bf16[1,2,8,64,128]{4,3,2,1,0:T(8,128)(2,1)}, u32[]{:S(2)}, u32[]{:S(2)}) collective-permute-start(bf16[1,2,8,64,128]{4,3,2,1,0:T(8,128)(2,1)} %get-tuple-element.369), channel_id=1, source_target_pairs={{0,4},{4,0},{8,12},{12,8},{16,20},{20,16},{24,28},{28,24},{1,5},{5... | collective-permute-start | bytes 786440 | tf_op jit(solution)/shard_map/cond/branch_5_fun/ppermute | solution.py:431
  73.0 6.0 %copy-start.17 = (bf16[1,512,768]{2,1,0:T(8,128)(2,1)S(1)}, bf16[1,512,768]{2,1,0:T(8,128)(2,1)}, u32[]{:S(2)}) copy-start(bf16[1,512,768]{2,1,0:T(8,128)(2,1)} %get-tuple-element.304) | copy-start | bytes 2359300 | tf_op jit(solution)/shard_map/cond
  73.0 59.2 %all-to-all-start.11 = ((bf16[8,4,5,64,128]{4,3,2,1,0:T(8,128)(2,1)}), bf16[8,4,5,64,128]{4,3,2,1,0:T(8,128)(2,1)}, u32[]{:S(2)}, u32[]{:S(2)}) async-start(bf16[8,4,5,64,128]{4,3,2,1,0:T(8,128)(2,1)} %temporal.10), calls=%async_computation.11 | async-start | bytes 5242880 | tf_op jit(solution)/shard_map/cond/branch_5_fun/all_to_all | solution.py:458
  85.0 45.0 %collective-permute-start.17 = (f32[1,2,512]{2,1,0:T(2,128)S(1)}, f32[1,2,512]{2,1,0:T(2,128)S(1)}, u32[]{:S(2)}, u32[]{:S(2)}) collective-permute-start(f32[1,2,512]{2,1,0:T(2,128)S(1)} %get-tuple-element.315), channel_id=1, source_target_pairs={{4,0},{8,4},{12,8},{16,12},{20,16},{24,20},{28,24},{5,1},{9,5},{13... | collective-permute-start | bytes 12296 | tf_op jit(solution)/shard_map/cond/branch_5_fun/ppermute | solution.py:418
